TPU v7x, 32 devices: a whole 2x2x4 slice. The times are simulated.
32 devices in a mesh: seq: 4 (over y, core), leaf: 8 (over z, x).
Axes of the slice: x: 2, y: 2, z: 4, core: 2. Of those that a mesh axis runs over, the one named last changes fastest.
Arguments:
- queries: bfloat16 [64, 4, 4096], P('leaf'), may hold values from -32 to 32
- prompt_kv: bfloat16 [2, 5120, 512], P(None, 'seq'), may hold values from -8 to 8
- node_kv: bfloat16 [2, 128, 256, 512], P(None, 'leaf', 'seq'), may hold values from -8 to 8
- node_lengths: int32 [128], P('leaf'), may hold values from 128 to 256, as said below
- ancestors: int32 [64, 10], P('leaf'), may hold values from -1 to 127, as said below
Outputs:
- attended: bfloat16 [64, 4, 4096], P('leaf', None, 'seq')
Inputs may be any that keep to these rules, and one draw needn't show every extreme that they name: `ancestors`: each entry is -1 or a node id, owner * 16 + slot, whose owner is an index of leaf. The last entry of every row is the leaf's own node, owned by the index of leaf that holds the leaf. A node whose owner is not the index of leaf holding the leaf sits in slot 15 of its owner, and each owner holds one such node at most. `node_lengths`: multiples of 128.
All inputs are finite; a program needn't handle non-finite values.
Results may differ from a plain program's by a relative error of at most 0.0028.
Values may be sent and summed in bfloat16 or wider, within the bound.
A program may use at most 64 MiB of HBM per device.

v0:
```python
import math

import jax
import jax.numpy as jnp
from jax import lax
from jax.sharding import PartitionSpec as P

HEADS = 16
KV_HEADS = 2
HEAD_DIM = 256


def joined(x, axis, combine):
    everything = jax.tree.map(lambda part: lax.all_gather(part, axis), x)
    initial = jax.tree.map(lambda part: part[0], everything)

    def hop(k, so_far):
        return combine(so_far, jax.tree.map(lambda part: part[k], everything))

    return lax.fori_loop(1, lax.axis_size(axis), hop, initial)


def combine_parts(first_part, second_part):
    first_max, first_total, first_sum = first_part
    second_max, second_total, second_sum = second_part
    top_max = jnp.maximum(first_max, second_max)
    first_weight = jnp.exp(first_max - top_max)
    second_weight = jnp.exp(second_max - top_max)
    return (
        top_max,
        first_total * first_weight + second_total * second_weight,
        first_sum * first_weight[..., None] + second_sum * second_weight[..., None],
    )


def shards(queries, prompt_kv, node_kv, node_lengths, ancestors):
    leaf_count, step_count, feat_width = queries.shape
    group_size = HEADS // KV_HEADS
    node_slots = node_kv.shape[1]
    token_count = node_kv.shape[2]
    level_count = ancestors.shape[1]
    score_scale = 1.0 / math.sqrt(HEAD_DIM)
    query_rows = queries.reshape(leaf_count, step_count, KV_HEADS, group_size, HEAD_DIM)
    prompt_keys = prompt_kv[0].reshape(-1, KV_HEADS, HEAD_DIM)
    prompt_values = prompt_kv[1].reshape(-1, KV_HEADS, HEAD_DIM)
    prompt_scores = (
        jnp.einsum("lskgd,pkd->lskgp", query_rows, prompt_keys, preferred_element_type=jnp.float32)
        * score_scale
    )
    shared_kv, shared_lengths = (
        lax.all_gather(node_kv[:, node_slots - 1 :], "leaf", axis=1, tiled=True),
        lax.all_gather(
            node_lengths[node_slots - 1 :].astype(jnp.bfloat16), "leaf", axis=0, tiled=True
        ),
    )
    kv_table = jnp.concatenate([node_kv, shared_kv], axis=1)
    length_table = jnp.concatenate([node_lengths, shared_lengths.astype(jnp.int32)])
    device_id = lax.axis_index("leaf")
    safe_ids = jnp.maximum(ancestors, 0)
    owner_dev = safe_ids // node_slots
    row_index = jnp.where(owner_dev == device_id, safe_ids % node_slots, node_slots + owner_dev)
    picked = kv_table[:, row_index]
    entries = jnp.arange(length_table.shape[0], dtype=jnp.int32)
    lengths = jnp.sum(jnp.where(row_index[..., None] == entries, length_table, 0), axis=-1)
    position = lax.axis_index("seq") * token_count + jnp.arange(token_count, dtype=jnp.int32)
    present = (ancestors >= 0)[:, :, None] & (position[None, None, :] < lengths[:, :, None])
    step_ids = jnp.arange(step_count, dtype=jnp.int32)
    own_limit = lengths[:, -1][:, None] - step_count + step_ids[None, :]
    last_level = jnp.arange(level_count, dtype=jnp.int32) == level_count - 1
    causal = jnp.logical_not(last_level)[None, None, :, None] | (
        position[None, None, None, :] <= own_limit[:, :, None, None]
    )
    allowed = present[:, None] & causal
    node_keys = picked[0].reshape(leaf_count, level_count, token_count, KV_HEADS, HEAD_DIM)
    node_values = picked[1].reshape(leaf_count, level_count, token_count, KV_HEADS, HEAD_DIM)
    node_scores = (
        jnp.einsum("lskgd,ljtkd->lskgjt", query_rows, node_keys, preferred_element_type=jnp.float32)
        * score_scale
    )
    node_scores = jnp.where(allowed[:, :, None, None], node_scores, -jnp.inf)
    block_max = jnp.maximum(jnp.max(prompt_scores, axis=-1), jnp.max(node_scores, axis=(-2, -1)))
    prompt_weights = jnp.exp(prompt_scores - block_max[..., None])
    node_weights = jnp.exp(node_scores - block_max[..., None, None])
    block_total = jnp.sum(prompt_weights, axis=-1) + jnp.sum(node_weights, axis=(-2, -1))
    block_sum = jnp.einsum(
        "lskgp,pkd->lskgd",
        prompt_weights.astype(jnp.bfloat16),
        prompt_values,
        preferred_element_type=jnp.float32,
    )
    block_sum = block_sum + jnp.einsum(
        "lskgjt,ljtkd->lskgd",
        node_weights.astype(jnp.bfloat16),
        node_values,
        preferred_element_type=jnp.float32,
    )
    columns = feat_width // lax.axis_size("seq")
    col_start = lax.axis_index("seq") * columns
    merged = joined((block_max, block_total, block_sum), "seq", combine_parts)
    denominator = merged[1]
    numerator = merged[2].reshape(leaf_count, step_count, feat_width)
    numerator = lax.dynamic_slice_in_dim(numerator, col_start, columns, 2)
    spread = jnp.broadcast_to(denominator[..., None], denominator.shape + (HEAD_DIM,)).reshape(
        leaf_count, step_count, feat_width
    )
    spread = lax.dynamic_slice_in_dim(spread, col_start, columns, 2)
    return (numerator / spread).astype(jnp.bfloat16)


def solution(mesh):
    placed = (
        P("leaf", None, None),
        P(None, "seq", None),
        P(None, "leaf", "seq", None),
        P("leaf"),
        P("leaf", None),
    )
    return jax.shard_map(
        shards, mesh=mesh, in_specs=placed, out_specs=P("leaf", None, "seq"), check_vma=False
    )
```

profile of v0, /device:TPU:1, one launch (start us, length us, event | category | flops | bytes accessed | tf_op | source)
XLA Modules:
  0.0 143.2 jit_solution(13837326270732787865)
XLA Ops:
  6.5 1.6 %slice.34 = bf16[2,1,64,512]{3,2,1,0:T(8,128)(2,1)} slice(bf16[2,16,64,512]{3,2,1,0:T(8,128)(2,1)} %param.9), slice={[0:2], [15:16], [0:64], [0:512]} | slice | bytes 262144 | tf_op jit(solution)/shard_map/slice | solution.py:51
  8.2 0.7 convert.3
  8.8 0.6 slice.32
  9.4 0.7 compare_select_fusion
  10.1 1.3 dynamic-slice
  11.4 1.4 dynamic-update-slice
  12.8 0.1 copy.79
  12.9 18.7 %all-reduce = bf16[8]{0:T(256)(128)(2,1)S(1)} all-reduce(bf16[8]{0:T(256)(128)(2,1)S(1)} %dynamic-update-slice), channel_id=1, replica_groups=mesh['seq'=4,'leaf'=8] {'leaf'}, use_global_device_ids=true, to_apply=%add | all-reduce | flops 8 | bytes 32
  31.6 0.7 pad_add_fusion
  32.3 0.3 select_reduce_fusion
  32.7 0.1 copy.80
  32.8 0.1 reshape.99
  32.8 1.1 reshape.94
  34.0 1.9 %fusion.39 = (bf16[1,1280,512]{2,1,0:T(8,128)(2,1)S(1)}, bf16[1,1280,512]{2,1,0:T(8,128)(2,1)S(1)}) fusion(bf16[2,1280,512]{2,1,0:T(8,128)(2,1)} %param.8), kind=kLoop, calls=%fused_computation.62 | loop fusion | bytes 5242880 | tf_op jit(solution)/shard_map/slice | solution.py:45
  35.9 1.5 %copy.121 = bf16[1,1280,512]{1,2,0:T(8,128)(2,1)} copy(bf16[1,1280,512]{2,1,0:T(8,128)(2,1)S(1)} %get-tuple-element.246) | data formatting | bytes 2621440
  37.3 1.4 copy.122
  38.8 0.1 iota_add_fusion
  38.8 0.1 broadcast_compare_fusion
  38.9 0.1 compare_and_fusion
  39.0 0.1 or_and_fusion
  39.2 2.1 %fusion.40 = (f32[8,4,2,8]{3,1,0,2:T(4,128)S(1)}, f32[8,4,2,8,1280]{4,3,1,0,2:T(8,128)}) fusion(bf16[1280,2,256,1,1]{0,2,4,3,1:T(8,128)(2,1)S(1)} %bitcast.85, bf16[8,4,2,8,256]{4,3,2,1,0:T(8,128)(2,1)S(1)} %reshape.94), kind=kOutput, calls=%fused_computation.63 | convolution fusion | flops 336854528 | bytes 4196352 | tf_op jit(solution)/shard_map/lskgd,pkd->lskgp/dot_general | solution.py:47
  41.2 9.7 %all-gather.6.cloned.1.call-done = bf16[2,8,64,512]{3,2,1,0:T(8,128)(2,1)} async-done(((bf16[2,1,64,512]{3,2,1,0:T(8,128)(2,1)}), bf16[2,8,64,512]{3,2,1,0:T(8,128)(2,1)}) %all-gather.6.cloned.1.call-update) | async-done | bytes 1048592 | tf_op jit(solution)/shard_map/all_gather | solution.py:51
  50.9 2.2 %pad_maximum_fusion = bf16[2,24,64,512]{3,2,1,0:T(8,128)(2,1)S(1)} fusion(bf16[2,8,64,512]{3,2,1,0:T(8,128)(2,1)} %all-gather.6.cloned.1.call-done, bf16[2,16,64,512]{3,2,1,0:T(8,128)(2,1)} %param.9), kind=kLoop, calls=%fused_computation.21 | loop fusion | flops 1572864 | bytes 6291456 | tf_op jit(solution)/shard_map/concatenate | solution.py:56
  53.1 6.1 %gather_fusion = bf16[80,2,64,512]{3,2,1,0:T(8,128)(2,1)} fusion(bf16[2,24,64,512]{3,2,1,0:T(8,128)(2,1)S(1)} %pad_maximum_fusion, s32[1024]{0:T(1024)S(1)} %pad_clamp_fusion), kind=kCustom, calls=%fused_computation | custom fusion | bytes 20971840 | tf_op jit(solution)/shard_map/gather | solution.py:62
  59.2 9.6 %copy.165 = bf16[8,10,2,64,512]{4,3,1,0,2:T(8,128)(2,1)} copy(bf16[8,10,2,64,512]{4,3,2,1,0:T(8,128)(2,1)} %bitcast.80) | data formatting | bytes 20971520 | tf_op jit(solution)/shard_map/gather | solution.py:62
  68.8 9.5 %fusion.38 = (bf16[1,8,10,64,512]{4,3,2,1,0:T(8,128)(2,1)}, bf16[1,8,10,64,512]{4,3,2,1,0:T(8,128)(2,1)}) fusion(bf16[2,8,10,64,512]{4,3,2,1,0:T(8,128)(2,1)} %bitcast.79), kind=kLoop, calls=%fused_computation.61 | loop fusion | bytes 20971520 | tf_op jit(solution)/shard_map/slice | solution.py:75
  78.3 8.3 %reshape_squeeze.13 = bf16[8,10,64,2,256]{4,3,2,1,0:T(2,128)(2,1)} reshape(bf16[1,8,10,64,512]{4,3,2,1,0:T(8,128)(2,1)} %get-tuple-element.242) | data formatting | bytes 10485760 | tf_op jit(solution)/shard_map/reshape;squeeze | solution.py:74
  86.6 5.0 %fusion.14 = (f32[8,4,2,8]{3,1,2,0:T(4,128)S(1)}, f32[8,2,10,64,4,8]{3,5,4,2,1,0:T(8,128)S(1)}) fusion(pred[8,4,10,64]{3,1,2,0:T(4,128)(4,1)S(1)} %or_and_fusion, bf16[8,10,64,2,256,1]{4,3,2,1,0,5:T(2,128)(2,1)} %bitcast.82, bf16[8,4,2,8,256]{4,3,2,1,0:T(8,128)(2,1)S(1)} %reshape.94), kind=kOutput, calls=%fused_computation.29 | convolution fusion | flops 168754688 | bytes 6838272 | tf_op jit(solution)/shard_map/lskgd,ljtkd->lskgjt/dot_general | solution.py:77
  91.7 8.3 %reshape_squeeze.15 = bf16[8,10,64,2,256]{4,3,2,1,0:T(2,128)(2,1)} reshape(bf16[1,8,10,64,512]{4,3,2,1,0:T(8,128)(2,1)} %get-tuple-element.241) | data formatting | bytes 10485760 | tf_op jit(solution)/shard_map/reshape;squeeze | solution.py:75
  100.0 0.9 fusion.12
  101.0 3.7 %fusion.25 = f32[8,4,2,8,256]{4,3,1,0,2:T(8,128)S(1)} fusion(bf16[8,4,2,8,10,64]{5,3,1,4,2,0:T(8,128)(2,1)S(1)} %get-tuple-element.243, bf16[8,10,64,2,256,1]{4,3,2,1,0,5:T(2,128)(2,1)} %bitcast.81), kind=kOutput, calls=%fused_computation.35 | convolution fusion | flops 167772160 | bytes 6422528 | tf_op jit(solution)/shard_map/lskgjt,ljtkd->lskgd/dot_general | solution.py:91
  104.7 1.4 fusion.22
  106.1 0.5 fusion.11
  106.6 6.9 %all-gather.1 = f32[32,4,2,8]{3,1,2,0:T(4,128)S(1)} all-gather(f32[8,4,2,8]{3,1,2,0:T(4,128)S(1)} %copy.91), channel_id=3, replica_groups=mesh['seq'=4,'leaf'=8] {'seq'}, dimensions={0}, use_global_device_ids=true | all-gather | bytes 10240 | tf_op jit(solution)/shard_map/all_gather | solution.py:14
  113.6 6.0 %all-gather = f32[32,4,2,8]{3,1,2,0:T(4,128)S(1)} all-gather(f32[8,4,2,8]{3,1,2,0:T(4,128)S(1)} %copy.86), channel_id=2, replica_groups=mesh['seq'=4,'leaf'=8] {'seq'}, dimensions={0}, use_global_device_ids=true | all-gather | bytes 10240 | tf_op jit(solution)/shard_map/all_gather | solution.py:14
  119.6 10.1 %all-gather.8.cloned.1.call-done = f32[32,4,2,8,256]{4,3,1,0,2:T(8,128)} async-done(((f32[8,4,2,8,256]{4,3,1,0,2:T(8,128)}), f32[32,4,2,8,256]{4,3,1,0,2:T(8,128)}) %all-gather.8.cloned.1.call-update) | async-done | bytes 2097168 | tf_op jit(solution)/shard_map/all_gather | solution.py:14
  129.7 1.1 slice.51
  130.8 4.3 %while.19 = (s32[]{:T(128)}, f32[8,4,2,8]{3,2,1,0:T(2,128)S(1)}, f32[8,4,2,8]{3,2,1,0:T(2,128)S(1)}, f32[8,4,2,8,256]{4,3,2,1,0:T(8,128)S(1)}, f32[4,8,4,2,8]{4,...) while((s32[]{:T(128)}, f32[8,4,2,8]{3,2,1,0:T(2,128)S(1)}, ...), condition=%wide.region_6.7_spmd, body=%wide.region_5.6_spmd.sunk | while | flops 396293 | bytes 1601687 | solution.py:20
  130.8 0.1 fusion.46
  130.9 1.3 fusion.47
  132.3 0.1 fusion.46
  132.4 1.3 fusion.47
  133.7 0.1 fusion.46
  133.8 1.3 fusion.47
  135.1 0.1 broadcast_in_dim.53
  135.2 0.2 reshape.96
  135.5 0.2 reshape.95
  135.7 0.7 fusion.32
  (32 shorter events, 0.3 us)
Async XLA Ops:
  6.5 44.4 %all-gather.6.cloned.1.call-start = ((), (), s32[]{:S(2)}) async-start(), calls=%async_computation | async-start | bytes 1179648 | tf_op jit(solution)/shard_map/all_gather | solution.py:51
  8.1 121.5 %all-gather.8.cloned.1.call-start = ((), (), s32[]{:S(2)}) async-start(), calls=%async_computation.1 | async-start | bytes 2621440 | tf_op jit(solution)/shard_map/all_gather | solution.py:14
  35.9 3.0 %copy-start.3 = (s32[8,10]{1,0:T(8,128)S(1)}, s32[8,10]{1,0:T(8,128)}, u32[]{:S(2)}) copy-start(s32[8,10]{1,0:T(8,128)} %param.11) | copy-start | bytes 964
  37.3 1.8 %copy-start.2 = (bf16[1,1280,512]{1,2,0:T(8,128)(2,1)S(1)}, bf16[1,1280,512]{1,2,0:T(8,128)(2,1)}, u32[]{:S(2)}) copy-start(bf16[1,1280,512]{1,2,0:T(8,128)(2,1)} %copy.121) | copy-start | bytes 3932164
  101.0 3.7 %copy-start = (f32[8,4,2,8,1280]{4,3,1,0,2:T(8,128)S(1)}, f32[8,4,2,8,1280]{4,3,1,0,2:T(8,128)}, u32[]{:S(2)}) copy-start(f32[8,4,2,8,1280]{4,3,1,0,2:T(8,128)} %get-tuple-element.250) | copy-start | bytes 7864324
  101.0 3.7 %copy-start.1 = (bf16[1,1280,512]{1,2,0:T(8,128)(2,1)S(1)}, bf16[1,1280,512]{1,2,0:T(8,128)(2,1)}, u32[]{:S(2)}) copy-start(bf16[1,1280,512]{1,2,0:T(8,128)(2,1)} %copy.122) | copy-start | bytes 3932164
Sparse Core Ops, SparseCore 0:
  9.5 41.3 all-gather.5
  106.2 23.4 all-gather.7
where the time goes:
time: 144 us; the launch traced here: 143 us
  local copies, waits for them, and re-layouts  54.7 us (38%)
  blocking collectives  31.6 us (22%)
  waiting for transfers between devices  19.8 us (14%)
  between operations  13.6 us (9%)
  matrix products  12.2 us (8%)
  other arithmetic  11.3 us (8%)
    unnamed x1, blocking collectives  18.7 us
    gather x2, local copies, waits for them, and re-layouts, shards(): picked = kv_table[:, row_index]  15.7 us
    all_gather x2, blocking collectives, joined(): everything = jax.tree.map(lambda part: lax.all_gather(part, axis), x)  12.9 us
    all_gather x1, waiting for transfers between devices, joined(): everything = jax.tree.map(lambda part: lax.all_gather(part, axis), x)  10.1 us
    all_gather x1, waiting for transfers between devices, shards(): lax.all_gather(node_kv[:, node_slots - 1:], 'leaf', axis=1, tiled=True)  9.67 us
    slice x1, local copies, waits for them, and re-layouts, shards(): picked[1].reshape(leaf_count, level_count, token_count, KV_HEADS, HEAD_DIM)  9.53 us
    another operation x1, local copies, waits for them, and re-layouts, shards(): picked[1].reshape(leaf_count, level_count, token_count, KV_HEADS, HEAD_DIM)  8.32 us
    another operation x1, local copies, waits for them, and re-layouts, shards(): picked[0].reshape(leaf_count, level_count, token_count, KV_HEADS, HEAD_DIM)  8.31 us
  transfers between devices with their start and end apart: 2, of which 2 were waited for; matrix products, arithmetic and copies ran while one was open for 10% of the time, Pallas kernels for 0%

commit v1 on v0

v1 whole, which is shorter than its diff:
```python
import functools
import math

import jax
import jax.numpy as jnp
from jax import lax
from jax.experimental import pallas as pl
from jax.experimental.pallas import tpu as pltpu
from jax.sharding import PartitionSpec as P

HEADS = 16
KV_HEADS = 2
HEAD_DIM = 256
GROUP = HEADS // KV_HEADS
HIDDEN = -1e30
LOG2E = 1.4426950408889634
MESH = pl.DeviceIdType.MESH


def scores_of(q, keys):
    dims = (((1,), (1,)), ((), ()))
    raw = lax.dot_general(q, keys, dims, preferred_element_type=jnp.float32)
    return raw * (LOG2E / math.sqrt(HEAD_DIM))


def biased(scores, bias):
    rows, cols = scores.shape
    per = bias.shape[0]
    return (scores.reshape(rows // per, per, cols) + bias[None]).reshape(rows, cols)


def bias_of(count):
    extra = jnp.where(count > 1.5, jnp.log(jnp.maximum(count, 1.0)) * LOG2E, 0.0)
    return jnp.where(count > 0.5, extra, HIDDEN)


def mix(p, values):
    return jnp.dot(p.astype(jnp.bfloat16), values, preferred_element_type=jnp.float32)


def merge(one, two):
    m1, l1, a1 = one
    m2, l2, a2 = two
    top = jnp.maximum(m1, m2)
    w1, w2 = jnp.exp2(m1 - top), jnp.exp2(m2 - top)
    return top, l1 * w1 + l2 * w2, a1 * w1 + a2 * w2


def packed(m, l):
    lane = lax.broadcasted_iota(jnp.int32, (m.shape[0], 128), 1)
    return jnp.where(lane == 0, m, jnp.where(lane == 1, l, 0.0))


def kernel(
    seq_size, leaf_size, steps,
    q_hbm, prompt_hbm, node_hbm, len_ref, anc_ref, out_ref,
    q_in, prompt, node, qs, shared, lens, bias_ref,
    acc, stat, stat_t, got_acc, got_stat, pair_out, pair_in,
    load_sem, slot_send, slot_recv, len_send, len_recv,
    block_send, block_recv, acc_send, acc_recv, stat_send, stat_recv, pair_sem,
):
    pairs = seq_size // 2
    per_kv = pairs // KV_HEADS
    pair_rows = (HEADS // pairs) * q_in.shape[0]
    half_rows = pair_rows // 2
    rows = q_in.shape[0]
    slots, tokens = node.shape[1], node.shape[2]
    levels = anc_ref.shape[1]
    far = leaf_size // 2
    seq, leaf = lax.axis_index("seq"), lax.axis_index("leaf")
    pair, core = seq // 2, lax.rem(seq, 2)
    kv = pair // per_kv
    place = lax.rem(pair, per_kv)
    line, side = leaf // 2, lax.rem(leaf, 2)
    sibling = (pair * 2 + 1 - core, leaf)
    across = (seq, line * 2 + 1 - side)

    def pair_at(p):
        return (p * 2 + core, leaf)

    def leaf_at(n):
        return (seq, n)

    def kv_cols(k):
        return pl.ds(pl.multiple_of(k * HEAD_DIM, HEAD_DIM), HEAD_DIM)

    loads = [
        pltpu.make_async_copy(q_hbm, q_in, load_sem.at[0]),
        pltpu.make_async_copy(node_hbm, node, load_sem.at[1]),
        pltpu.make_async_copy(prompt_hbm, prompt, load_sem.at[2]),
    ]
    for load in loads:
        load.start()

    barrier = pltpu.get_barrier_semaphore()
    for d in range(1, pairs):
        pl.semaphore_signal(barrier, inc=1, device_id=pair_at(lax.rem(pair + d, pairs)), device_id_type=MESH)
    for d in range(1, leaf_size):
        pl.semaphore_signal(barrier, inc=1, device_id=leaf_at(lax.rem(leaf + d, leaf_size)), device_id_type=MESH)
    pl.semaphore_signal(barrier, inc=1, device_id=sibling, device_id_type=MESH)
    lens[pl.ds(leaf, 1)] = jnp.full((1, 8, 128), len_ref[slots - 1], jnp.int32)
    pl.semaphore_wait(barrier, pairs + leaf_size - 1)

    slot_copies = []
    for d in range(1, pairs):
        to = lax.rem(pair + d, pairs)
        slot_copies.append(pltpu.make_async_remote_copy(
            src_ref=node_hbm.at[:, slots - 1, :, kv_cols(to // per_kv)],
            dst_ref=shared.at[leaf, :, pair],
            send_sem=slot_send.at[d], recv_sem=slot_recv.at[d],
            device_id=pair_at(to), device_id_type=MESH,
        ))
        slot_copies[-1].start()
    own_slot = pltpu.make_async_copy(
        node_hbm.at[:, slots - 1, :, kv_cols(kv)], shared.at[leaf, :, pair], load_sem.at[3]
    )
    own_slot.start()
    len_copies = []
    for d in range(1, leaf_size):
        len_copies.append(pltpu.make_async_remote_copy(
            src_ref=lens.at[leaf], dst_ref=lens.at[leaf],
            send_sem=len_send.at[d], recv_sem=len_recv.at[d],
            device_id=leaf_at(lax.rem(leaf + d, leaf_size)), device_id_type=MESH,
        ))
        len_copies[-1].start()

    loads[0].wait()
    for h in range(HEADS):
        qs[h // GROUP, (h % GROUP) * rows:(h % GROUP + 1) * rows, :] = q_in[:, h * HEAD_DIM:(h + 1) * HEAD_DIM]

    for copy in slot_copies:
        copy.wait_recv()
    own_slot.wait()

    def block_copy(source, target, n):
        return pltpu.make_async_remote_copy(
            src_ref=shared.at[source], dst_ref=shared.at[source],
            send_sem=block_send.at[n], recv_sem=block_recv.at[n],
            device_id=target, device_id_type=MESH,
        )

    own_across = block_copy(leaf, across, 0)
    own_across.start()
    along = []
    for d in range(1, far):
        along.append(block_copy(leaf, leaf_at(lax.rem(line + d, far) * 2 + side), d))
        along[-1].start()

    anc = jnp.zeros((rows, levels), jnp.int32)
    row_leaf = lax.broadcasted_iota(jnp.int32, (rows, levels), 0) // steps
    for n in range(rows // steps):
        anc = jnp.where(row_leaf == n, anc_ref[n:n + 1, :], anc)
    width = slots * tokens
    col = lax.broadcasted_iota(jnp.int32, (1, width), 1)
    col_slot = col // tokens
    position = seq * tokens + col - col_slot * tokens
    held = jnp.zeros((1, width), jnp.int32)
    for n in range(slots):
        held = jnp.where(col_slot == n, len_ref[n], held)
    ident = leaf * slots + col_slot
    inside = position < held
    count = jnp.zeros((rows, width), jnp.float32)
    for level in range(levels - 1):
        count += jnp.where(anc[:, level:level + 1] == ident, 1.0, 0.0)
    step = lax.rem(lax.broadcasted_iota(jnp.int32, (rows, width), 0), steps)
    last = (anc[:, levels - 1:] == ident) & (position <= held - steps + step)
    count += jnp.where(last, 1.0, 0.0)
    bias_ref[...] = bias_of(jnp.where(inside, count, 0.0))

    loads[1].wait()
    loads[2].wait()

    def main(k, n):
        q = qs[k]
        cols = kv_cols(k)
        first = scores_of(q, prompt[0, :, cols])
        second = biased(scores_of(q, node[0, :, :, cols].reshape(width, HEAD_DIM)), bias_ref[...])
        m = jnp.maximum(jnp.max(first, axis=1, keepdims=True), jnp.max(second, axis=1, keepdims=True))
        first = jnp.exp2(first - m)
        second = jnp.exp2(second - m)
        l = jnp.sum(first, axis=1, keepdims=True) + jnp.sum(second, axis=1, keepdims=True)
        acc[n] = mix(first, prompt[1, :, cols]) + mix(second, node[1, :, :, cols].reshape(width, HEAD_DIM))
        both = packed(m, l)
        stat[n] = both
        stat_t[n] = both.T[:8]

    def send_part(n, place_there, to, slot):
        part = pl.ds(pl.multiple_of(place_there * pair_rows, pair_rows), pair_rows)
        copies = [
            pltpu.make_async_remote_copy(
                src_ref=acc.at[n, part], dst_ref=got_acc.at[slot],
                send_sem=acc_send.at[slot], recv_sem=acc_recv.at[slot],
                device_id=pair_at(to), device_id_type=MESH,
            ),
            pltpu.make_async_remote_copy(
                src_ref=stat_t.at[n], dst_ref=got_stat.at[slot],
                send_sem=stat_send.at[slot], recv_sem=stat_recv.at[slot],
                device_id=pair_at(to), device_id_type=MESH,
            ),
        ]
        for copy in copies:
            copy.start()
        return copies

    forwards = []

    def forward(d):
        along[d - 1].wait_recv()
        source = lax.rem(line + far - d, far) * 2 + side
        forwards.append(block_copy(source, across, far + d - 1))
        forwards[-1].start()

    main(1 - kv, 0)
    parts = []
    for n in range(per_kv):
        place_there = lax.rem(place + n, per_kv)
        parts += send_part(0, place_there, (1 - kv) * per_kv + place_there, n)
    forward(1)
    main(kv, 1)
    for n in range(1, per_kv):
        place_there = lax.rem(place + n, per_kv)
        parts += send_part(1, place_there, kv * per_kv + place_there, per_kv + n - 1)

    mine = pl.ds(pl.multiple_of(place * pair_rows, pair_rows), pair_rows)
    q_mine = qs[kv, mine]
    state = (stat[1, mine, 0:1], stat[1, mine, 1:2], acc[1, mine])

    for copy in len_copies:
        copy.wait_recv()
    span = pairs * tokens
    span_col = lax.broadcasted_iota(jnp.int32, (1, span), 1)
    span_block = span_col // tokens
    span_position = (span_block * 2 + core) * tokens + span_col - span_block * tokens

    def visit(state, source):
        m, l, total = state
        target = source * slots + slots - 1
        count = jnp.zeros((rows, 1), jnp.float32)
        for level in range(levels - 1):
            count += jnp.where(anc[:, level:level + 1] == target, 1.0, 0.0)
        bias = bias_of(jnp.where(span_position < lens[source][0:1, :span], count, 0.0))
        s = biased(scores_of(q_mine, shared[source, 0].reshape(span, HEAD_DIM)), bias)
        top = jnp.maximum(m, jnp.max(s, axis=1, keepdims=True))
        p = jnp.exp2(s - top)
        w = jnp.exp2(m - top)
        return (
            top,
            l * w + jnp.sum(p, axis=1, keepdims=True),
            total * w + mix(p, shared[source, 1].reshape(span, HEAD_DIM)),
        )

    def line_source(d, s):
        return lax.rem(line + far - d, far) * 2 + s

    for d in range(2, far):
        forward(d)
        if d == 2:
            own_across.wait_recv()
            state = visit(state, line_source(0, 1 - side))
        state = visit(state, line_source(d - 1, side))
    state = visit(state, line_source(far - 1, side))

    for n in range(pairs - 1):
        parts[2 * n].wait_recv()
        parts[2 * n + 1].wait_recv()
        stats = jnp.concatenate([got_stat[n], jnp.zeros((120, GROUP * rows), jnp.float32)], axis=0).T
        stat[0] = stats
        state = merge(state, (stat[0, mine, 0:1], stat[0, mine, 1:2], got_acc[n]))

    for d in range(1, far):
        forwards[d - 1].wait_recv()
        state = visit(state, line_source(d, 1 - side))

    pair_out[:, HEAD_DIM:] = packed(state[0], state[1])
    pair_out[:, :HEAD_DIM] = state[2]

    def half(n):
        return pl.ds(pl.multiple_of(n * half_rows, half_rows), half_rows)

    swap = pltpu.make_async_remote_copy(
        src_ref=pair_out.at[half(1 - core)], dst_ref=pair_in,
        send_sem=pair_sem.at[0], recv_sem=pair_sem.at[1],
        device_id=sibling, device_id_type=MESH,
    )
    swap.start()
    kept = pair_out[half(core)]
    swap.wait_recv()
    came = pair_in[...]
    _, l, total = merge(
        (kept[:, HEAD_DIM:HEAD_DIM + 1], kept[:, HEAD_DIM + 1:HEAD_DIM + 2], kept[:, :HEAD_DIM]),
        (came[:, HEAD_DIM:HEAD_DIM + 1], came[:, HEAD_DIM + 1:HEAD_DIM + 2], came[:, :HEAD_DIM]),
    )
    result = (total / l).astype(out_ref.dtype)
    for h in range(half_rows // rows):
        out_ref[:, h * HEAD_DIM:(h + 1) * HEAD_DIM] = result[h * rows:(h + 1) * rows]

    for copy in slot_copies + len_copies + [own_across] + along + forwards + parts + [swap]:
        copy.wait_send()


def shards(seq_size, leaf_size, queries, prompt_kv, node_kv, node_lengths, ancestors):
    leaves, steps, feats = queries.shape
    rows = leaves * steps
    slots, tokens, wide = node_kv.shape[1:]
    pairs = seq_size // 2
    pair_rows = (HEADS // pairs) * rows
    span = pairs * tokens
    kv_rows = GROUP * rows
    dma = pltpu.SemaphoreType.DMA
    out = pl.pallas_call(
        functools.partial(kernel, seq_size, leaf_size, steps),
        out_shape=jax.ShapeDtypeStruct((rows, feats // seq_size), jnp.bfloat16),
        in_specs=[pl.BlockSpec(memory_space=pl.ANY)] * 3
        + [pl.BlockSpec(memory_space=pltpu.SMEM), pl.BlockSpec(memory_space=pltpu.VMEM)],
        out_specs=pl.BlockSpec(memory_space=pltpu.VMEM),
        scratch_shapes=[
            pltpu.VMEM((rows, feats), jnp.bfloat16),
            pltpu.VMEM(prompt_kv.shape, jnp.bfloat16),
            pltpu.VMEM(node_kv.shape, jnp.bfloat16),
            pltpu.VMEM((KV_HEADS, kv_rows, HEAD_DIM), jnp.bfloat16),
            pltpu.VMEM((leaf_size, 2, pairs, tokens, HEAD_DIM), jnp.bfloat16),
            pltpu.VMEM((leaf_size, 8, 128), jnp.int32),
            pltpu.VMEM((rows, slots * tokens), jnp.float32),
            pltpu.VMEM((2, kv_rows, HEAD_DIM), jnp.float32),
            pltpu.VMEM((2, kv_rows, 128), jnp.float32),
            pltpu.VMEM((2, 8, kv_rows), jnp.float32),
            pltpu.VMEM((pairs - 1, pair_rows, HEAD_DIM), jnp.float32),
            pltpu.VMEM((pairs - 1, 8, kv_rows), jnp.float32),
            pltpu.VMEM((pair_rows, HEAD_DIM + 128), jnp.float32),
            pltpu.VMEM((pair_rows // 2, HEAD_DIM + 128), jnp.float32),
            dma((4,)),
            dma((pairs,)), dma((pairs,)),
            dma((leaf_size,)), dma((leaf_size,)),
            dma((leaf_size,)), dma((leaf_size,)),
            dma((pairs,)), dma((pairs,)),
            dma((pairs,)), dma((pairs,)),
            dma((2,)),
        ],
        compiler_params=pltpu.CompilerParams(
            collective_id=0, has_side_effects=True, vmem_limit_bytes=48 * 1024 * 1024
        ),
    )(queries.reshape(rows, feats), prompt_kv, node_kv, node_lengths, ancestors)
    return out.reshape(leaves, steps, feats // seq_size)


def solution(mesh):
    placed = (
        P("leaf", None, None),
        P(None, "seq", None),
        P(None, "leaf", "seq", None),
        P("leaf"),
        P("leaf", None),
    )
    return jax.shard_map(
        functools.partial(shards, mesh.shape["seq"], mesh.shape["leaf"]),
        mesh=mesh, in_specs=placed, out_specs=P("leaf", None, "seq"), check_vma=False,
    )
```

time: 144 us -> 34.6 us (0.24)
  local copies, waits for them, and re-layouts: 54.7 us -> 6.34 us
  blocking collectives: 31.6 us -> 0 us
  Pallas kernels: 0 us -> 27.5 us
  waiting for transfers between devices: 19.8 us -> 0 us
  between operations: 13.6 us -> 0.03 us
  matrix products: 12.2 us -> 0 us
  other arithmetic: 11.3 us -> 0 us
    pallas_call x0 -> x1, Pallas kernels: none -> 27.5 us  [shards(): pl.pallas_call(functools.partial(kernel, seq_size, leaf_size, steps), out...]
    all_gather x2 -> x0, waiting for transfers between devices: 19.8 us -> none  [the longest x1 10.1 us: joined(): everything = jax.tree.map(lambda part: lax.all_gather(part, axis), x)]
    unnamed x1 -> x0, blocking collectives: 18.7 us -> none
    another operation x2 -> x0, local copies, waits for them, and re-layouts: 16.6 us -> none  [the longest x1 8.32 us: shards(): picked[1].reshape(leaf_count, level_count, token_count, KV_HEADS, HEAD_DIM)]
    gather x2 -> x0, local copies, waits for them, and re-layouts: 15.7 us -> none  [shards(): picked = kv_table[:, row_index]]
    slice x7 -> x0, local copies, waits for them, and re-layouts: 14.6 us -> none  [the longest x1 9.53 us: shards(): picked[1].reshape(leaf_count, level_count, token_count, KV_HEADS, HEAD_DIM)]
    all_gather x2 -> x0, blocking collectives: 12.9 us -> none  [joined(): everything = jax.tree.map(lambda part: lax.all_gather(part, axis), x)]
    dot_general x4 -> x0, matrix products: 12.2 us -> none  [the longest x1 5.05 us: shards(): jnp.einsum('lskgd,ljtkd->lskgjt', query_rows, node_keys, preferred_elemen...]
  transfers between devices with their start and end apart: 2 -> 0, of which waited for: 2 -> 0; matrix products, arithmetic and copies ran while one was open for 10% -> 0% of each run, Pallas kernels for 0% -> 0%
where the time goes in v1:
time: 34.6 us; the launch traced here: 33.9 us
  Pallas kernels  27.5 us (79%)
  local copies, waits for them, and re-layouts  6.34 us (18%)
    pallas_call x1, Pallas kernels, shards(): pl.pallas_call(functools.partial(kernel, seq_size, leaf_size, steps), out...  27.5 us
    unnamed x8, local copies, waits for them, and re-layouts  4.67 us
    reshape x1, local copies, waits for them, and re-layouts, shards(): queries.reshape(rows, feats)  1.01 us

profile of v1, /device:TPU:1, one launch (start us, length us, event | category | flops | bytes accessed | tf_op | source)
XLA Modules:
  0.0 33.9 jit_solution(14453157349431347843)
XLA Ops:
  0.0 1.0 %reshape.6.q_hbm = bf16[32,4096]{1,0:T(8,128)(2,1)S(1)} reshape(bf16[8,4,4096]{2,1,0:T(4,128)(2,1)} %param.5) | data formatting | bytes 524288 | tf_op jit(solution)/shard_map/reshape | solution.py:342
  1.0 0.0 copy-start
  1.0 1.7 %copy-done = bf16[2,1280,512]{2,1,0:T(8,128)(2,1)S(1)} copy-done((bf16[2,1280,512]{2,1,0:T(8,128)(2,1)S(1)}, bf16[2,1280,512]{2,1,0:T(8,128)(2,1)}, u32[]{:S(2)}) %copy-start) | copy-done | bytes 2621464
  2.8 0.0 copy-start.1
  2.8 1.6 %copy-done.1 = bf16[2,16,64,512]{3,2,1,0:T(8,128)(2,1)S(1)} copy-done((bf16[2,16,64,512]{3,2,1,0:T(8,128)(2,1)S(1)}, bf16[2,16,64,512]{3,2,1,0:T(8,128)(2,1)}, u32[]{:S(2)}) %copy-start.1) | copy-done | bytes 2097176
  4.4 0.0 copy-start.2
  4.4 0.7 %copy-done.2 = s32[8,10]{1,0:T(8,128)S(1)} copy-done((s32[8,10]{1,0:T(8,128)S(1)}, s32[8,10]{1,0:T(8,128)}, u32[]{:S(2)}) %copy-start.2) | copy-done | bytes 344
  5.0 0.0 copy-start.3
  5.0 0.7 %copy-done.3 = s32[16]{0:T(128)S(1)} copy-done((s32[16]{0:T(128)S(1)}, s32[16]{0:T(128)}, u32[]{:S(2)}) %copy-start.3) | copy-done | bytes 88
  5.7 27.5 %shard_map.55 = bf16[32,1024]{1,0:T(8,128)(2,1)S(1)} custom-call(bf16[32,4096]{1,0:T(8,128)(2,1)S(1)} %reshape.6.q_hbm, bf16[2,1280,512]{2,1,0:T(8,128)(2,1)S(1)} %copy-done, bf16[2,16,64,512]{3,2,1,0:T(8,128)(2,1)S(1)} %copy-done.1, s32[16]{0:T(128)S(1)} %copy-done.3, s32[8,10]{1,0:T(8,128)S(1)} %copy-done.2), custom_call_target="tpu_custom_call" | custom-call | tf_op jit(solution)/shard_map/pallas_call | solution.py:310
  33.2 0.7 %reshape.7 = bf16[8,4,1024]{2,1,0:T(4,128)(2,1)} reshape(bf16[32,1024]{1,0:T(8,128)(2,1)S(1)} %shard_map.55) | data formatting | bytes 131072 | tf_op jit(solution)/shard_map/reshape | solution.py:343
Async XLA Ops:
  1.0 1.7 %copy-start = (bf16[2,1280,512]{2,1,0:T(8,128)(2,1)S(1)}, bf16[2,1280,512]{2,1,0:T(8,128)(2,1)}, u32[]{:S(2)}) copy-start(bf16[2,1280,512]{2,1,0:T(8,128)(2,1)} %prompt_hbm.1) | copy-start | bytes 7864324
  2.8 1.6 %copy-start.1 = (bf16[2,16,64,512]{3,2,1,0:T(8,128)(2,1)S(1)}, bf16[2,16,64,512]{3,2,1,0:T(8,128)(2,1)}, u32[]{:S(2)}) copy-start(bf16[2,16,64,512]{3,2,1,0:T(8,128)(2,1)} %node_hbm.1) | copy-start | bytes 6291460
  4.4 0.7 %copy-start.2 = (s32[8,10]{1,0:T(8,128)S(1)}, s32[8,10]{1,0:T(8,128)}, u32[]{:S(2)}) copy-start(s32[8,10]{1,0:T(8,128)} %anc_ref.1) | copy-start | bytes 964
  5.0 0.7 %copy-start.3 = (s32[16]{0:T(128)S(1)}, s32[16]{0:T(128)}, u32[]{:S(2)}) copy-start(s32[16]{0:T(128)} %len_ref.1) | copy-start | bytes 196

commit v2 on v1

--- a/solution.py
+++ b/solution.py
@@ -53,17 +53,17 @@
 
 def kernel(
     seq_size, leaf_size, steps,
-    q_hbm, prompt_hbm, node_hbm, len_ref, anc_ref, out_ref,
-    q_in, prompt, node, qs, shared, lens, bias_ref,
+    q_hbm, prompt_hbm, node_hbm, len_hbm, anc_hbm, out_ref,
+    q_in, q_rows, prompt, node, len_ref, anc_ref, qs, shared, lens, bias_ref,
     acc, stat, stat_t, got_acc, got_stat, pair_out, pair_in,
     load_sem, slot_send, slot_recv, len_send, len_recv,
-    block_send, block_recv, acc_send, acc_recv, stat_send, stat_recv, pair_sem,
+    across_send, up_send, down_send, block_recv, acc_send, acc_recv, stat_send, stat_recv, pair_sem,
 ):
     pairs = seq_size // 2
     per_kv = pairs // KV_HEADS
-    pair_rows = (HEADS // pairs) * q_in.shape[0]
+    rows = q_rows.shape[0]
+    pair_rows = (HEADS // pairs) * rows
     half_rows = pair_rows // 2
-    rows = q_in.shape[0]
     slots, tokens = node.shape[1], node.shape[2]
     levels = anc_ref.shape[1]
     far = leaf_size // 2
@@ -89,7 +89,14 @@
         pltpu.make_async_copy(node_hbm, node, load_sem.at[1]),
         pltpu.make_async_copy(prompt_hbm, prompt, load_sem.at[2]),
     ]
-    for load in loads:
+    own_slot = pltpu.make_async_copy(
+        node_hbm.at[:, slots - 1, :, kv_cols(kv)], shared.at[leaf, :, pair], load_sem.at[3]
+    )
+    small = [
+        pltpu.make_async_copy(len_hbm, len_ref, load_sem.at[4]),
+        pltpu.make_async_copy(anc_hbm, anc_ref, load_sem.at[5]),
+    ]
+    for load in [own_slot] + small + loads:
         load.start()
 
     barrier = pltpu.get_barrier_semaphore()
@@ -98,6 +105,8 @@
     for d in range(1, leaf_size):
         pl.semaphore_signal(barrier, inc=1, device_id=leaf_at(lax.rem(leaf + d, leaf_size)), device_id_type=MESH)
     pl.semaphore_signal(barrier, inc=1, device_id=sibling, device_id_type=MESH)
+    for load in small:
+        load.wait()
     lens[pl.ds(leaf, 1)] = jnp.full((1, 8, 128), len_ref[slots - 1], jnp.int32)
     pl.semaphore_wait(barrier, pairs + leaf_size - 1)
 
@@ -111,10 +120,67 @@
             device_id=pair_at(to), device_id_type=MESH,
         ))
         slot_copies[-1].start()
-    own_slot = pltpu.make_async_copy(
-        node_hbm.at[:, slots - 1, :, kv_cols(kv)], shared.at[leaf, :, pair], load_sem.at[3]
-    )
-    own_slot.start()
+
+    def piece_copy(source, e, target, sems):
+        piece = shared.at[source, :, lax.rem(pair + e, pairs)]
+        return pltpu.make_async_remote_copy(
+            src_ref=piece, dst_ref=piece,
+            send_sem=sems.at[source, e], recv_sem=block_recv.at[source, e],
+            device_id=target, device_id_type=MESH,
+        )
+
+    up, down = leaf_at(leaf + 2), leaf_at(leaf - 2)
+    can_up, can_down = line < far - 1, line > 0
+
+    def send_own(e):
+        @pl.when(can_up)
+        def _():
+            piece_copy(leaf, e, up, up_send).start()
+
+        @pl.when(can_down)
+        def _():
+            piece_copy(leaf, e, down, down_send).start()
+
+        piece_copy(leaf, e, across, across_send).start()
+
+    def pass_on(t, e):
+        @pl.when(line >= t)
+        def _():
+            source = leaf - 2 * t
+            piece_copy(source, e, down, up_send).wait_recv()
+
+            @pl.when(can_up)
+            def _():
+                piece_copy(source, e, up, up_send).start()
+
+            piece_copy(source, e, across, across_send).start()
+
+        @pl.when(line + t < far)
+        def _():
+            source = leaf + 2 * t
+            piece_copy(source, e, up, down_send).wait_recv()
+
+            @pl.when(can_down)
+            def _():
+                piece_copy(source, e, down, down_send).start()
+
+            piece_copy(source, e, across, across_send).start()
+
+    def wait_sent(e):
+        for n in range(far):
+            source = 2 * n + side
+            piece_copy(source, e, across, across_send).wait_send()
+
+            @pl.when((line >= n) & can_up)
+            def _():
+                piece_copy(source, e, up, up_send).wait_send()
+
+            @pl.when((line <= n) & can_down)
+            def _():
+                piece_copy(source, e, down, down_send).wait_send()
+
+    own_slot.wait()
+    send_own(0)
     len_copies = []
     for d in range(1, leaf_size):
         len_copies.append(pltpu.make_async_remote_copy(
@@ -125,26 +191,16 @@
         len_copies[-1].start()
 
     loads[0].wait()
+    for n in range(rows // steps):
+        q_rows[n * steps:(n + 1) * steps, :] = q_in[n].astype(jnp.float32)
     for h in range(HEADS):
-        qs[h // GROUP, (h % GROUP) * rows:(h % GROUP + 1) * rows, :] = q_in[:, h * HEAD_DIM:(h + 1) * HEAD_DIM]
-
-    for copy in slot_copies:
-        copy.wait_recv()
-    own_slot.wait()
-
-    def block_copy(source, target, n):
-        return pltpu.make_async_remote_copy(
-            src_ref=shared.at[source], dst_ref=shared.at[source],
-            send_sem=block_send.at[n], recv_sem=block_recv.at[n],
-            device_id=target, device_id_type=MESH,
+        qs[h // GROUP, (h % GROUP) * rows:(h % GROUP + 1) * rows, :] = (
+            q_rows[:, h * HEAD_DIM:(h + 1) * HEAD_DIM].astype(jnp.bfloat16)
         )
 
-    own_across = block_copy(leaf, across, 0)
-    own_across.start()
-    along = []
-    for d in range(1, far):
-        along.append(block_copy(leaf, leaf_at(lax.rem(line + d, far) * 2 + side), d))
-        along[-1].start()
+    for d in range(1, pairs):
+        slot_copies[pairs - 1 - d].wait_recv()
+        send_own(d)
 
     anc = jnp.zeros((rows, levels), jnp.int32)
     row_leaf = lax.broadcasted_iota(jnp.int32, (rows, levels), 0) // steps
@@ -202,21 +258,19 @@
             copy.start()
         return copies
 
-    forwards = []
-
-    def forward(d):
-        along[d - 1].wait_recv()
-        source = lax.rem(line + far - d, far) * 2 + side
-        forwards.append(block_copy(source, across, far + d - 1))
-        forwards[-1].start()
-
+    pass_on(1, 0)
     main(1 - kv, 0)
     parts = []
     for n in range(per_kv):
         place_there = lax.rem(place + n, per_kv)
         parts += send_part(0, place_there, (1 - kv) * per_kv + place_there, n)
-    forward(1)
+    for e in range(1, pairs):
+        pass_on(1, e)
+    pass_on(2, 0)
     main(kv, 1)
+    for e in range(1, pairs):
+        pass_on(2, e)
+    pass_on(3, 0)
     for n in range(1, per_kv):
         place_there = lax.rem(place + n, per_kv)
         parts += send_part(1, place_there, kv * per_kv + place_there, per_kv + n - 1)
@@ -249,16 +303,26 @@
             total * w + mix(p, shared[source, 1].reshape(span, HEAD_DIM)),
         )
 
-    def line_source(d, s):
-        return lax.rem(line + far - d, far) * 2 + s
-
-    for d in range(2, far):
-        forward(d)
-        if d == 2:
-            own_across.wait_recv()
-            state = visit(state, line_source(0, 1 - side))
-        state = visit(state, line_source(d - 1, side))
-    state = visit(state, line_source(far - 1, side))
+    def nearest(n):
+        short = jnp.minimum(line, far - 1 - line)
+        off = jnp.where(n < 2 * short, n // 2 + 1, n + 1 - short)
+        below = jnp.where(n < 2 * short, n % 2 == 0, 2 * line > far - 1)
+        return jnp.where(below, line - off, line + off) * 2
+
+    def visit_across(state, source):
+        for e in range(pairs):
+            piece_copy(source, e, across, across_send).wait_recv()
+        return visit(state, source)
+
+    state = visit_across(state, line * 2 + 1 - side)
+    state = visit(state, nearest(0) + side)
+    for e in range(1, pairs):
+        pass_on(3, e)
+    for t in range(4, far):
+        for e in range(pairs):
+            pass_on(t, e)
+    for n in range(1, far - 1):
+        state = visit(state, nearest(n) + side)
 
     for n in range(pairs - 1):
         parts[2 * n].wait_recv()
@@ -267,9 +331,8 @@
         stat[0] = stats
         state = merge(state, (stat[0, mine, 0:1], stat[0, mine, 1:2], got_acc[n]))
 
-    for d in range(1, far):
-        forwards[d - 1].wait_recv()
-        state = visit(state, line_source(d, 1 - side))
+    for n in range(far - 1):
+        state = visit_across(state, nearest(n) + 1 - side)
 
     pair_out[:, HEAD_DIM:] = packed(state[0], state[1])
     pair_out[:, :HEAD_DIM] = state[2]
@@ -294,7 +357,9 @@
     for h in range(half_rows // rows):
         out_ref[:, h * HEAD_DIM:(h + 1) * HEAD_DIM] = result[h * rows:(h + 1) * rows]
 
-    for copy in slot_copies + len_copies + [own_across] + along + forwards + parts + [swap]:
+    for e in range(pairs):
+        wait_sent(e)
+    for copy in slot_copies + len_copies + parts + [swap]:
         copy.wait_send()
 
 
@@ -310,13 +375,15 @@
     out = pl.pallas_call(
         functools.partial(kernel, seq_size, leaf_size, steps),
         out_shape=jax.ShapeDtypeStruct((rows, feats // seq_size), jnp.bfloat16),
-        in_specs=[pl.BlockSpec(memory_space=pl.ANY)] * 3
-        + [pl.BlockSpec(memory_space=pltpu.SMEM), pl.BlockSpec(memory_space=pltpu.VMEM)],
+        in_specs=[pl.BlockSpec(memory_space=pl.ANY)] * 5,
         out_specs=pl.BlockSpec(memory_space=pltpu.VMEM),
         scratch_shapes=[
-            pltpu.VMEM((rows, feats), jnp.bfloat16),
+            pltpu.VMEM(queries.shape, jnp.bfloat16),
+            pltpu.VMEM((rows, feats), jnp.float32),
             pltpu.VMEM(prompt_kv.shape, jnp.bfloat16),
             pltpu.VMEM(node_kv.shape, jnp.bfloat16),
+            pltpu.SMEM(node_lengths.shape, jnp.int32),
+            pltpu.VMEM(ancestors.shape, jnp.int32),
             pltpu.VMEM((KV_HEADS, kv_rows, HEAD_DIM), jnp.bfloat16),
             pltpu.VMEM((leaf_size, 2, pairs, tokens, HEAD_DIM), jnp.bfloat16),
             pltpu.VMEM((leaf_size, 8, 128), jnp.int32),
@@ -328,18 +395,19 @@
             pltpu.VMEM((pairs - 1, 8, kv_rows), jnp.float32),
             pltpu.VMEM((pair_rows, HEAD_DIM + 128), jnp.float32),
             pltpu.VMEM((pair_rows // 2, HEAD_DIM + 128), jnp.float32),
-            dma((4,)),
+            dma((6,)),
             dma((pairs,)), dma((pairs,)),
             dma((leaf_size,)), dma((leaf_size,)),
-            dma((leaf_size,)), dma((leaf_size,)),
+            dma((leaf_size, pairs)), dma((leaf_size, pairs)),
+            dma((leaf_size, pairs)), dma((leaf_size, pairs)),
             dma((pairs,)), dma((pairs,)),
             dma((pairs,)), dma((pairs,)),
             dma((2,)),
         ],
         compiler_params=pltpu.CompilerParams(
-            collective_id=0, has_side_effects=True, vmem_limit_bytes=48 * 1024 * 1024
+            collective_id=0, has_side_effects=True, vmem_limit_bytes=121 * 512 * 1024
         ),
-    )(queries.reshape(rows, feats), prompt_kv, node_kv, node_lengths, ancestors)
+    )(queries, prompt_kv, node_kv, node_lengths, ancestors)
     return out.reshape(leaves, steps, feats // seq_size)
 
 

time: 34.6 us -> 27 us (0.78); the launches traced: 33.9 us -> 26.9 us
  local copies, waits for them, and re-layouts: 6.34 us -> 1.5 us
  Pallas kernels: 27.5 us -> 25.4 us
    unnamed x8 -> x0, local copies, waits for them, and re-layouts: 4.67 us -> none
    pallas_call x1, Pallas kernels: 27.5 us -> 25.4 us  [shards(): pl.pallas_call(functools.partial(kernel, seq_size, leaf_size, steps), out...]
    reshape x1 -> x0, local copies, waits for them, and re-layouts: 1.01 us -> none  [shards(): queries.reshape(rows, feats)]
    reshape x1, local copies, waits for them, and re-layouts: 0.66 us -> 1.5 us  [shards(): return out.reshape(leaves, steps, feats // seq_size)]
where the time goes in v2:
time: 27 us; the launch traced here: 26.9 us
  Pallas kernels  25.4 us (94%)
  local copies, waits for them, and re-layouts  1.5 us (6%)
    pallas_call x1, Pallas kernels, shards(): pl.pallas_call(functools.partial(kernel, seq_size, leaf_size, steps), out...  25.4 us
    reshape x1, local copies, waits for them, and re-layouts, shards(): return out.reshape(leaves, steps, feats // seq_size)  1.5 us

profile of v2, /device:TPU:1, one launch (start us, length us, event | category | flops | bytes accessed | tf_op | source)
XLA Modules:
  0.0 26.9 jit_solution(15832301837221194442)
XLA Ops:
  0.0 25.4 %shard_map.55 = bf16[32,1024]{1,0:T(8,128)(2,1)} custom-call(bf16[8,4,4096]{2,1,0:T(4,128)(2,1)} %q_hbm.1, bf16[2,1280,512]{2,1,0:T(8,128)(2,1)} %prompt_hbm.1, bf16[2,16,64,512]{3,2,1,0:T(8,128)(2,1)} %node_hbm.1, s32[16]{0:T(128)} %len_hbm.1, s32[8,10]{1,0:T(8,128)} %anc_hbm.1), custom_call_target="tpu_custom_call" | custom-call | tf_op jit(solution)/shard_map/pallas_call | solution.py:375
  25.4 1.5 %reshape.3 = bf16[8,4,1024]{2,1,0:T(4,128)(2,1)} reshape(bf16[32,1024]{1,0:T(8,128)(2,1)} %shard_map.55) | data formatting | bytes 131072 | tf_op jit(solution)/shard_map/reshape | solution.py:411

commit v3 on v2

--- a/solution.py
+++ b/solution.py
@@ -226,7 +226,7 @@
     loads[1].wait()
     loads[2].wait()
 
-    def main(k, n):
+    def weigh(k):
         q = qs[k]
         cols = kv_cols(k)
         first = scores_of(q, prompt[0, :, cols])
@@ -235,6 +235,11 @@
         first = jnp.exp2(first - m)
         second = jnp.exp2(second - m)
         l = jnp.sum(first, axis=1, keepdims=True) + jnp.sum(second, axis=1, keepdims=True)
+        return first.astype(jnp.bfloat16), second.astype(jnp.bfloat16), m, l
+
+    def add_up(k, n, weighed):
+        first, second, m, l = weighed
+        cols = kv_cols(k)
         acc[n] = mix(first, prompt[1, :, cols]) + mix(second, node[1, :, :, cols].reshape(width, HEAD_DIM))
         both = packed(m, l)
         stat[n] = both
@@ -259,21 +264,23 @@
         return copies
 
     pass_on(1, 0)
-    main(1 - kv, 0)
+    weighed = weigh(1 - kv)
+    for e in range(1, pairs):
+        pass_on(1, e)
+    add_up(1 - kv, 0, weighed)
     parts = []
     for n in range(per_kv):
         place_there = lax.rem(place + n, per_kv)
         parts += send_part(0, place_there, (1 - kv) * per_kv + place_there, n)
-    for e in range(1, pairs):
-        pass_on(1, e)
     pass_on(2, 0)
-    main(kv, 1)
+    weighed = weigh(kv)
     for e in range(1, pairs):
         pass_on(2, e)
-    pass_on(3, 0)
+    add_up(kv, 1, weighed)
     for n in range(1, per_kv):
         place_there = lax.rem(place + n, per_kv)
         parts += send_part(1, place_there, kv * per_kv + place_there, per_kv + n - 1)
+    pass_on(3, 0)
 
     mine = pl.ds(pl.multiple_of(place * pair_rows, pair_rows), pair_rows)
     q_mine = qs[kv, mine]
@@ -315,9 +322,9 @@
         return visit(state, source)
 
     state = visit_across(state, line * 2 + 1 - side)
-    state = visit(state, nearest(0) + side)
     for e in range(1, pairs):
         pass_on(3, e)
+    state = visit(state, nearest(0) + side)
     for t in range(4, far):
         for e in range(pairs):
             pass_on(t, e)
@@ -353,9 +360,11 @@
         (kept[:, HEAD_DIM:HEAD_DIM + 1], kept[:, HEAD_DIM + 1:HEAD_DIM + 2], kept[:, :HEAD_DIM]),
         (came[:, HEAD_DIM:HEAD_DIM + 1], came[:, HEAD_DIM + 1:HEAD_DIM + 2], came[:, :HEAD_DIM]),
     )
-    result = (total / l).astype(out_ref.dtype)
+    result = total / l
     for h in range(half_rows // rows):
-        out_ref[:, h * HEAD_DIM:(h + 1) * HEAD_DIM] = result[h * rows:(h + 1) * rows]
+        q_rows[:, h * HEAD_DIM:(h + 1) * HEAD_DIM] = result[h * rows:(h + 1) * rows]
+    for n in range(rows // steps):
+        out_ref[n] = q_rows[n * steps:(n + 1) * steps, :out_ref.shape[2]].astype(out_ref.dtype)
 
     for e in range(pairs):
         wait_sent(e)
@@ -372,9 +381,9 @@
     span = pairs * tokens
     kv_rows = GROUP * rows
     dma = pltpu.SemaphoreType.DMA
-    out = pl.pallas_call(
+    return pl.pallas_call(
         functools.partial(kernel, seq_size, leaf_size, steps),
-        out_shape=jax.ShapeDtypeStruct((rows, feats // seq_size), jnp.bfloat16),
+        out_shape=jax.ShapeDtypeStruct((leaves, steps, feats // seq_size), jnp.bfloat16),
         in_specs=[pl.BlockSpec(memory_space=pl.ANY)] * 5,
         out_specs=pl.BlockSpec(memory_space=pltpu.VMEM),
         scratch_shapes=[
@@ -408,7 +417,6 @@
             collective_id=0, has_side_effects=True, vmem_limit_bytes=121 * 512 * 1024
         ),
     )(queries, prompt_kv, node_kv, node_lengths, ancestors)
-    return out.reshape(leaves, steps, feats // seq_size)
 
 
 def solution(mesh):

time: 27 us -> 27 us (level)
    reshape x1 -> x0, local copies, waits for them, and re-layouts: 1.5 us -> none  [shards(): return out.reshape(leaves, steps, feats // seq_size)]
    unnamed x0 -> x1, local copies, waits for them, and re-layouts: none -> 1.49 us
where the time goes in v3:
time: 27 us; the launch traced here: 26.9 us
  Pallas kernels  25.4 us (94%)
  local copies, waits for them, and re-layouts  1.49 us (6%)
    pallas_call x1, Pallas kernels, shards(): pl.pallas_call(functools.partial(kernel, seq_size, leaf_size, steps), out...  25.4 us
    unnamed x1, local copies, waits for them, and re-layouts  1.49 us

profile of v3, /device:TPU:1, one launch (start us, length us, event | category | flops | bytes accessed | tf_op | source)
XLA Modules:
  0.0 26.9 jit_solution(9008356550198684691)
XLA Ops:
  0.0 25.4 %shard_map.55 = bf16[8,4,1024]{2,1,0:T(4,128)(2,1)} custom-call(bf16[8,4,4096]{2,1,0:T(4,128)(2,1)} %q_hbm.1, bf16[2,1280,512]{2,1,0:T(8,128)(2,1)} %prompt_hbm.1, bf16[2,16,64,512]{3,2,1,0:T(8,128)(2,1)} %node_hbm.1, s32[16]{0:T(128)} %len_hbm.1, s32[8,10]{1,0:T(8,128)} %anc_hbm.1), custom_call_target="tpu_custom_call" | custom-call | tf_op jit(solution)/shard_map/pallas_call | solution.py:384
  25.4 1.5 %copy.7 = bf16[8,4,1024]{2,1,0:T(4,128)(2,1)} copy(bf16[8,4,1024]{2,1,0:T(4,128)(2,1)} %shard_map.55) | data formatting | bytes 131072

commit v4 on v3

--- a/solution.py
+++ b/solution.py
@@ -263,9 +263,8 @@
             copy.start()
         return copies
 
-    pass_on(1, 0)
     weighed = weigh(1 - kv)
-    for e in range(1, pairs):
+    for e in range(pairs):
         pass_on(1, e)
     add_up(1 - kv, 0, weighed)
     parts = []

time: 27 us -> 27.3 us (1.011)
  Pallas kernels: 25.4 us -> 25.7 us
    pallas_call x1, Pallas kernels: 25.4 us -> 25.7 us  [shards(): pl.pallas_call(functools.partial(kernel, seq_size, leaf_size, steps), out...]
where the time goes in v4:
time: 27.3 us; the launch traced here: 27.2 us
  Pallas kernels  25.7 us (94%)
  local copies, waits for them, and re-layouts  1.49 us (5%)
    pallas_call x1, Pallas kernels, shards(): pl.pallas_call(functools.partial(kernel, seq_size, leaf_size, steps), out...  25.7 us
    unnamed x1, local copies, waits for them, and re-layouts  1.49 us

profile of v4, /device:TPU:1, one launch (start us, length us, event | category | flops | bytes accessed | tf_op | source)
XLA Modules:
  0.0 27.2 jit_solution(10958948847535157682)
XLA Ops:
  0.0 25.7 %shard_map.55 = bf16[8,4,1024]{2,1,0:T(4,128)(2,1)} custom-call(bf16[8,4,4096]{2,1,0:T(4,128)(2,1)} %q_hbm.1, bf16[2,1280,512]{2,1,0:T(8,128)(2,1)} %prompt_hbm.1, bf16[2,16,64,512]{3,2,1,0:T(8,128)(2,1)} %node_hbm.1, s32[16]{0:T(128)} %len_hbm.1, s32[8,10]{1,0:T(8,128)} %anc_hbm.1), custom_call_target="tpu_custom_call" | custom-call | tf_op jit(solution)/shard_map/pallas_call | solution.py:383
  25.7 1.5 %copy.7 = bf16[8,4,1024]{2,1,0:T(4,128)(2,1)} copy(bf16[8,4,1024]{2,1,0:T(4,128)(2,1)} %shard_map.55) | data formatting | bytes 131072
